TPU v7x, 32 devices: a whole 2x2x4 slice. The times are simulated.
32 devices in a mesh: group: 2 (over y), outer: 2 (over core), inner: 8 (over z, x).
Axes of the slice: x: 2, y: 2, z: 4, core: 2. Of those that a mesh axis runs over, the one named last changes fastest.
Arguments:
- queries: bfloat16 [16384, 384], P(('group', 'outer', 'inner')), parts along dimension 0, may hold values from -6 to 6
- key_rows: bfloat16 [16384, 384], P(('group', 'outer', 'inner')), parts along dimension 0, may hold values from -6 to 6
- value_rows: bfloat16 [16384, 384], P(('group', 'outer', 'inner')), parts along dimension 0, may hold values from -6 to 6
- grad_out: bfloat16 [16384, 384], P(('group', 'outer', 'inner')), parts along dimension 0, may hold values from -96 to 96
Outputs:
- attended: bfloat16 [16384, 384], P(('group', 'outer', 'inner')), parts along dimension 0
- grad_query: bfloat16 [16384, 384], P(('group', 'outer', 'inner')), parts along dimension 0
- grad_key: bfloat16 [16384, 384], P(('group', 'outer', 'inner')), parts along dimension 0
- grad_value: bfloat16 [16384, 384], P(('group', 'outer', 'inner')), parts along dimension 0
There are 2 independent parts, one for each index of `group`. A program takes and returns all parts, laid end to end along the dimension named above; each array names one. Nothing has to cross between parts.
All inputs are finite; a program needn't handle non-finite values.
Results may differ from a plain program's by a relative error of at most 0.0071.
Values may be sent and summed in bfloat16 or wider, within the bound.
A program may use at most 64 MiB of HBM per device.

v0:
```python
import jax
import jax.numpy as jnp
from jax import lax
from jax.sharding import PartitionSpec as P

E = 64
W1 = 512
R1 = 4
W2 = 8192
R2 = 64
KEYS = 512


NEGATIVE = -1e30


def product(form, left, right):
    return jnp.einsum(form, left, right, preferred_element_type=jnp.float32)


def pick(matrix, stride):
    length = matrix.shape[0]
    count = matrix.shape[1]
    folded = matrix.reshape((length // stride, stride) + matrix.shape[1:])
    return jnp.stack([folded[:, head % stride, head] for head in range(count)], axis=1)


def spread(matrix, stride, filler):
    count = matrix.shape[1]
    extra = (1,) * (matrix.ndim - 2)
    selector = (jnp.arange(stride)[:, None] == jnp.arange(count)[None, :] % stride).reshape(
        (1, stride, count) + extra
    )
    placed = jnp.where(selector, matrix[:, None], filler)
    return placed.reshape((matrix.shape[0] * stride,) + matrix.shape[1:])


def part_stats(query_sel, key_sel, value_sel):
    scale = query_sel.shape[-1] ** (-0.5)
    scores = product("qhe,khe->hqk", query_sel, key_sel) * scale
    peak = jnp.max(scores, axis=-1)
    weights = jnp.exp(scores - peak[..., None])
    mass = jnp.sum(weights, axis=-1)
    summed = product("hqk,khe->qhe", weights.astype(jnp.bfloat16), value_sel)
    return (peak.T, mass.T, summed)


def part_grads(query_sel, key_sel, value_sel, grad_sel, log_sel, dot_sel):
    scale = query_sel.shape[-1] ** (-0.5)
    scores = product("qhe,khe->hqk", query_sel, key_sel) * scale
    weights = jnp.exp(scores - log_sel.T[:, :, None])
    grad_v = product("hqk,qhe->khe", weights.astype(jnp.bfloat16), grad_sel)
    grad_w = product("qhe,khe->hqk", grad_sel, value_sel)
    grad_s = (weights * (grad_w - dot_sel.T[:, :, None]) * scale).astype(jnp.bfloat16)
    grad_q = product("hqk,khe->qhe", grad_s, key_sel)
    grad_k = product("hqk,qhe->khe", grad_s, query_sel)
    return (grad_q, grad_k, grad_v)


def run_stats(items):
    return part_stats(*items)


def run_grads(items):
    return part_grads(*items)


def shards(queries, key_rows, value_rows, grad_out):
    rows = queries.shape[0]
    width = queries.shape[1]
    heads = width // E
    devices_all = lax.axis_size("outer") * lax.axis_size("inner")
    stride_far = rows * devices_all // KEYS
    span = W2 // rows
    per_device = rows // R2
    near_count = rows // W1
    slide_pos = lax.axis_index(("outer", "inner"))
    query_heads = queries.reshape(rows, heads, E)
    key_heads = key_rows.reshape(rows, heads, E)
    value_heads = value_rows.reshape(rows, heads, E)
    grad_heads = grad_out.reshape(rows, heads, E)
    mid_pair = jnp.stack(
        [
            pick(key_heads, R2).reshape(per_device, width),
            pick(value_heads, R2).reshape(per_device, width),
        ]
    )
    far_pair = jnp.stack(
        [
            pick(key_heads, stride_far).reshape(-1, width),
            pick(value_heads, stride_far).reshape(-1, width),
        ]
    )
    first_row = slide_pos // span * (span * per_device)
    slide_mid, slide_far = (
        lax.all_gather(mid_pair, ("outer", "inner"), axis=1, tiled=True),
        lax.all_gather(far_pair, ("outer", "inner"), axis=1, tiled=True),
    )
    segment_pair = lax.dynamic_slice_in_dim(slide_mid, first_row, span * per_device, 1)
    key_mid = segment_pair[0].reshape(-1, heads, E)
    value_mid = segment_pair[1].reshape(-1, heads, E)
    key_far = slide_far[0].reshape(-1, heads, E)
    value_far = slide_far[1].reshape(-1, heads, E)

    def near_rows(matrix):
        return pick(matrix, R1).reshape((near_count, W1 // R1) + matrix.shape[1:])

    query_near = near_rows(query_heads)
    key_near = near_rows(key_heads)
    value_near = near_rows(value_heads)
    query_mid = pick(query_heads, R2)
    query_far = pick(query_heads, stride_far)
    peak_near, mass_near, summed_near = lax.map(run_stats, (query_near, key_near, value_near))
    peak_mid, mass_mid, summed_mid = part_stats(query_mid, key_mid, value_mid)
    peak_far, mass_far, summed_far = part_stats(query_far, key_far, value_far)
    branches = (
        (
            peak_near.reshape(-1, heads),
            mass_near.reshape(-1, heads),
            summed_near.reshape(-1, heads, E),
            R1,
        ),
        (peak_mid, mass_mid, summed_mid, R2),
        (peak_far, mass_far, summed_far, stride_far),
    )
    peak_list = [spread(item[0], item[3], NEGATIVE) for item in branches]
    peak_all = jnp.maximum(jnp.maximum(peak_list[0], peak_list[1]), peak_list[2])
    denom = jnp.zeros((rows, heads), jnp.float32)
    numer = jnp.zeros((rows, heads, E), jnp.float32)
    for branch in range(3):
        factor = jnp.exp(peak_list[branch] - peak_all)
        denom = denom + spread(branches[branch][1], branches[branch][3], 0.0) * factor
        numer = numer + spread(branches[branch][2], branches[branch][3], 0.0) * factor[..., None]
    position = jnp.arange(rows)[:, None]
    head_ids = jnp.arange(heads)[None, :]
    covered = (
        (position % R1 == head_ids % R1)
        | (position % R2 == head_ids % R2)
        | (position % stride_far == head_ids % stride_far)
    )
    safe = jnp.where(covered, denom, 1.0)
    result = jnp.where(covered[..., None], numer / safe[..., None], 0.0)
    log_total = peak_all + jnp.log(safe)
    dot_total = jnp.sum(grad_heads.astype(jnp.float32) * result, axis=-1)
    gq_near, gk_near, gv_near = lax.map(
        run_grads,
        (
            query_near,
            key_near,
            value_near,
            near_rows(grad_heads),
            near_rows(log_total),
            near_rows(dot_total),
        ),
    )
    gq_mid, gk_mid, gv_mid = part_grads(
        query_mid,
        key_mid,
        value_mid,
        pick(grad_heads, R2),
        pick(log_total, R2),
        pick(dot_total, R2),
    )
    gq_far, gk_far, gv_far = part_grads(
        query_far,
        key_far,
        value_far,
        pick(grad_heads, stride_far),
        pick(log_total, stride_far),
        pick(dot_total, stride_far),
    )
    mid_grads = jnp.stack([gk_mid.reshape(-1, width), gv_mid.reshape(-1, width)])
    far_grads = jnp.stack([gk_far.reshape(-1, width), gv_far.reshape(-1, width)])
    padded = jnp.zeros((2, devices_all * per_device, width), jnp.float32)
    padded = lax.dynamic_update_slice_in_dim(padded, mid_grads, first_row, 1)
    own_mid, own_far = (
        lax.psum_scatter(padded, ("outer", "inner"), scatter_dimension=1, tiled=True),
        lax.psum_scatter(far_grads, ("outer", "inner"), scatter_dimension=1, tiled=True),
    )
    grad_q = (
        spread(gq_near.reshape(-1, heads, E), R1, 0.0)
        + spread(gq_mid, R2, 0.0)
        + spread(gq_far, stride_far, 0.0)
    )
    grad_k = (
        spread(gk_near.reshape(-1, heads, E), R1, 0.0)
        + spread(own_mid[0].reshape(-1, heads, E), R2, 0.0)
        + spread(own_far[0].reshape(-1, heads, E), stride_far, 0.0)
    )
    grad_v = (
        spread(gv_near.reshape(-1, heads, E), R1, 0.0)
        + spread(own_mid[1].reshape(-1, heads, E), R2, 0.0)
        + spread(own_far[1].reshape(-1, heads, E), stride_far, 0.0)
    )
    return (
        result.reshape(rows, width).astype(jnp.bfloat16),
        grad_q.reshape(rows, width).astype(jnp.bfloat16),
        grad_k.reshape(rows, width).astype(jnp.bfloat16),
        grad_v.reshape(rows, width).astype(jnp.bfloat16),
    )


def solution(mesh):
    return jax.shard_map(
        shards,
        mesh=mesh,
        in_specs=(
            P(("group", "outer", "inner"), None),
            P(("group", "outer", "inner"), None),
            P(("group", "outer", "inner"), None),
            P(("group", "outer", "inner"), None),
        ),
        out_specs=(
            P(("group", "outer", "inner"), None),
            P(("group", "outer", "inner"), None),
            P(("group", "outer", "inner"), None),
            P(("group", "outer", "inner"), None),
        ),
        check_vma=False,
    )
```

profile of v0, /device:TPU:0, one launch (start us, length us, event | category | flops | bytes accessed | tf_op | source)
XLA Modules:
  0.0 362.5 jit_solution(17496458464297403014)
XLA Ops:
  7.2 2.5 reshape_reshape.44
  10.7 1.6 reshape_reshape.43
  13.2 1.5 reshape_reshape.42
  14.7 1.5 reshape.825
  16.3 1.6 reshape_reshape.36
  17.8 1.5 reshape_reshape.37
  26.3 1.6 reshape_reshape.45
  32.7 40.7 %all_gather.7 = bf16[2,512,384]{2,1,0:T(8,128)(2,1)S(1)} all-gather(bf16[2,32,384]{2,1,0:T(8,128)(2,1)S(1)} %pad_maximum_fusion.2), channel_id=1, replica_groups=mesh['group'=2,'outer'=2,'inner'=8] {'outer','inner'}, dimensions={1}, use_global_device_ids=true | all-gather | bytes 835584 | tf_op jit(solution)/shard_map/all_gather | solution.py:97
  74.3 1.7 fusion.135
  77.8 1.5 reshape_reshape.41
  86.0 1.5 reshape_reshape.40
  94.2 29.7 %all_gather.6 = bf16[2,128,384]{2,1,0:T(8,128)(2,1)S(1)} all-gather(bf16[2,8,384]{2,1,0:T(8,128)(2,1)S(1)} %pad_maximum_fusion.3), channel_id=1, replica_groups=mesh['group'=2,'outer'=2,'inner'=8] {'outer','inner'}, dimensions={1}, use_global_device_ids=true | all-gather | bytes 208896 | tf_op jit(solution)/shard_map/all_gather | solution.py:96
  124.6 1.5 fusion.134
  126.8 1.8 fusion.132
  145.8 2.6 broadcast_select_fusion
  152.7 1.5 reshape_reshape.47
  156.6 1.8 fusion.133
  159.0 1.8 fusion.130
  171.5 1.4 broadcast_in_dim.608
  174.2 1.8 copy.907
  176.0 2.4 broadcast_in_dim.592
  178.5 2.8 copy.955
  182.8 2.1 fusion.25
  186.3 2.2 fusion.138
  188.5 1.6 copy.1052
  191.4 1.6 copy.1053
  193.0 1.6 copy.1054
  197.3 1.9 fusion.61
  212.1 1.7 slice_reduce_fusion.18
  215.9 3.0 copy.984
  222.6 10.3 %copy.983 = f32[1,512,384]{2,0,1:T(1,128)} copy(f32[1,512,384]{1,2,0:T(8,128)S(1)} %bitcast.471) | data formatting | bytes 1572864 | tf_op jit(solution)/shard_map/stack;reshape | solution.py:173
  234.0 3.9 %pad_maximum_fusion = f32[2,512,384]{2,0,1:T(2,128)} fusion(f32[1,512,384]{2,0,1:T(1,128)} %copy.984, f32[1,512,384]{2,0,1:T(1,128)} %copy.983), kind=kLoop, calls=%fused_computation.12 | loop fusion | flops 393216 | bytes 3145728 | tf_op jit(solution)/shard_map/stack | solution.py:173
  245.5 1.4 broadcast_in_dim.613
  246.8 1.4 copy.947
  249.5 1.4 broadcast_in_dim.593
  250.9 1.5 copy.909
  260.7 2.3 copy.979
  263.5 1.4 broadcast_in_dim.661
  264.8 2.3 copy.976
  271.6 1.4 broadcast_in_dim.644
  273.0 2.3 copy.960
  275.3 60.0 %all-reduce.5.cloned.1.call-done = (f32[2,128,384]{2,0,1:T(2,128)}, f32[2,512,384]{2,0,1:T(2,128)}) async-done(((f32[2,128,384]{2,0,1:T(2,128)}, f32[2,512,384]{2,0,1:T(2,128)}), (f32[2,128,384]{2,0,1:T(2,128)}, f32[2,512,384]{2,0,1:T(2,128)})) %all-reduce.5.cloned.1.call-update) | async-done | bytes 1966096
  338.0 1.4 dynamic-slice_reduce_fusion
  339.6 1.4 broadcast_in_dim.677
  341.0 2.3 copy.990
  343.6 1.4 broadcast_in_dim.669
  344.9 2.3 copy.985
  349.1 3.5 fusion.22
  (426 shorter events, 121.4 us)
Async XLA Ops:
  7.2 3.5 copy-start.1
  7.2 328.1 %all-reduce.5.cloned.1.call-start = ((), (), s32[]{:S(2)}) async-start(), calls=%async_computation | async-start | bytes 3932160
  9.7 3.4 copy-start.3
  17.8 8.5 %copy-start.2 = (bf16[512,384]{1,0:T(8,128)(2,1)S(1)}, bf16[512,384]{1,0:T(8,128)(2,1)}, u32[]{:S(2)}) copy-start(bf16[512,384]{1,0:T(8,128)(2,1)} %param.7) | copy-start | bytes 1179652
  20.5 8.9 %copy-start.73 = (s32[6]{0:T(128)}, s32[6]{0:T(128)S(1)}, u32[]{:S(2)}) copy-start(s32[6]{0:T(128)S(1)} %get-tuple-element.236) | copy-start | bytes 76
  21.8 7.6 %copy-start.75 = (pred[16,6]{0,1:T(8,128)(4,1)}, pred[16,6]{0,1:T(8,128)(4,1)S(1)}, u32[]{:S(2)}) copy-start(pred[16,6]{0,1:T(8,128)(4,1)S(1)} %iota_compare_fusion) | copy-start | bytes 292
  23.4 6.0 %copy-start.74 = (pred[64,6]{0,1:T(8,128)(4,1)}, pred[64,6]{0,1:T(8,128)(4,1)S(1)}, u32[]{:S(2)}) copy-start(pred[64,6]{0,1:T(8,128)(4,1)S(1)} %iota_compare_fusion.1) | copy-start | bytes 1156
  123.9 9.3 %copy-start.71 = (s32[6]{0:T(128)S(1)}, s32[6]{0:T(128)}, u32[]{:S(2)}) copy-start(s32[6]{0:T(128)} %and_select_fusion.2) | copy-start | bytes 76
  123.9 9.9 %copy-start.31 = (bf16[32,6,64]{2,0,1:T(8,128)(2,1)S(1)}, bf16[32,6,64]{2,0,1:T(8,128)(2,1)}, u32[]{:S(2)}) copy-start(bf16[32,6,64]{2,0,1:T(8,128)(2,1)} %constant_dynamic-update-slice_fusion.41) | copy-start | bytes 73732
  123.9 9.9 %copy-start.56 = (bf16[32,1,1,64]{3,2,1,0:T(2,128)(2,1)S(1)}, bf16[32,1,1,64]{3,2,1,0:T(2,128)(2,1)}, u32[]{:S(2)}) copy-start(bf16[32,1,1,64]{3,2,1,0:T(2,128)(2,1)} %get-tuple-element.173) | copy-start | bytes 12292
  123.9 10.0 %copy-start.55 = (bf16[32,1,1,64]{3,2,1,0:T(2,128)(2,1)S(1)}, bf16[32,1,1,64]{3,2,1,0:T(2,128)(2,1)}, u32[]{:S(2)}) copy-start(bf16[32,1,1,64]{3,2,1,0:T(2,128)(2,1)} %get-tuple-element.172) | copy-start | bytes 12292
  124.6 9.3 %copy-start.54 = (bf16[32,1,1,64]{3,2,1,0:T(2,128)(2,1)S(1)}, bf16[32,1,1,64]{3,2,1,0:T(2,128)(2,1)}, u32[]{:S(2)}) copy-start(bf16[32,1,1,64]{3,2,1,0:T(2,128)(2,1)} %get-tuple-element.171) | copy-start | bytes 12292
  124.6 9.3 %copy-start.53 = (bf16[32,1,1,64]{3,2,1,0:T(2,128)(2,1)S(1)}, bf16[32,1,1,64]{3,2,1,0:T(2,128)(2,1)}, u32[]{:S(2)}) copy-start(bf16[32,1,1,64]{3,2,1,0:T(2,128)(2,1)} %get-tuple-element.170) | copy-start | bytes 12292
  124.6 9.4 %copy-start.52 = (bf16[32,1,1,64]{3,2,1,0:T(2,128)(2,1)S(1)}, bf16[32,1,1,64]{3,2,1,0:T(2,128)(2,1)}, u32[]{:S(2)}) copy-start(bf16[32,1,1,64]{3,2,1,0:T(2,128)(2,1)} %get-tuple-element.169) | copy-start | bytes 12292
  126.8 14.8 %copy-start.12 = (bf16[1,128,384]{1,2,0:T(8,128)(2,1)}, bf16[1,128,384]{1,2,0:T(8,128)(2,1)S(1)}, u32[]{:S(2)}) copy-start(bf16[1,128,384]{1,2,0:T(8,128)(2,1)S(1)} %copy.933) | copy-start | bytes 294916
  132.6 12.4 %copy-start.59 = (bf16[128,1,1,64]{0,3,2,1:T(8,128)(2,1)S(1)}, bf16[128,1,1,64]{0,3,2,1:T(8,128)(2,1)}, u32[]{:S(2)}) copy-start(bf16[128,1,1,64]{0,3,2,1:T(8,128)(2,1)} %copy.1023) | copy-start | bytes 49156
  132.6 12.4 %copy-start.60 = (bf16[128,1,1,64]{0,3,2,1:T(8,128)(2,1)S(1)}, bf16[128,1,1,64]{0,3,2,1:T(8,128)(2,1)}, u32[]{:S(2)}) copy-start(bf16[128,1,1,64]{0,3,2,1:T(8,128)(2,1)} %copy.1024) | copy-start | bytes 49156
  132.6 12.4 %copy-start.58 = (bf16[128,1,1,64]{0,3,2,1:T(8,128)(2,1)S(1)}, bf16[128,1,1,64]{0,3,2,1:T(8,128)(2,1)}, u32[]{:S(2)}) copy-start(bf16[128,1,1,64]{0,3,2,1:T(8,128)(2,1)} %copy.1025) | copy-start | bytes 49156
  132.6 12.4 %copy-start.57 = (bf16[128,1,1,64]{0,3,2,1:T(8,128)(2,1)S(1)}, bf16[128,1,1,64]{0,3,2,1:T(8,128)(2,1)}, u32[]{:S(2)}) copy-start(bf16[128,1,1,64]{0,3,2,1:T(8,128)(2,1)} %copy.1026) | copy-start | bytes 49156
  132.6 12.5 %copy-start.61 = (bf16[128,1,1,64]{0,3,2,1:T(8,128)(2,1)S(1)}, bf16[128,1,1,64]{0,3,2,1:T(8,128)(2,1)}, u32[]{:S(2)}) copy-start(bf16[128,1,1,64]{0,3,2,1:T(8,128)(2,1)} %copy.1027) | copy-start | bytes 49156
  134.0 11.5 %copy-start.32 = (bf16[32,6,64]{2,0,1:T(8,128)(2,1)}, bf16[32,6,64]{2,0,1:T(8,128)(2,1)S(1)}, u32[]{:S(2)}) copy-start(bf16[32,6,64]{2,0,1:T(8,128)(2,1)S(1)} %constant_dynamic-update-slice_fusion.36) | copy-start | bytes 73732
  134.0 11.8 %copy-start.24 = (pred[128,4,6]{1,0,2:T(8,128)(4,1)S(1)}, pred[128,4,6]{1,0,2:T(8,128)(4,1)}, u32[]{:S(2)}) copy-start(pred[128,4,6]{1,0,2:T(8,128)(4,1)} %broadcast_in_dim.627) | copy-start | bytes 9220
  134.0 11.8 %copy-start.25 = (pred[128,4,6]{1,0,2:T(8,128)(4,1)S(1)}, pred[128,4,6]{1,0,2:T(8,128)(4,1)}, u32[]{:S(2)}) copy-start(pred[128,4,6]{1,0,2:T(8,128)(4,1)} %broadcast_in_dim.623) | copy-start | bytes 9220
  134.3 29.6 %copy-start.42 = (f32[6,32]{1,0:T(8,128)}, f32[6,32]{1,0:T(8,128)S(1)}, u32[]{:S(2)}) copy-start(f32[6,32]{1,0:T(8,128)S(1)} %get-tuple-element.225) | copy-start | bytes 2308
  134.5 7.1 %copy-start.50 = (f32[6,32]{1,0:T(8,128)}, f32[6,32]{1,0:T(8,128)S(1)}, u32[]{:S(2)}) copy-start(f32[6,32]{1,0:T(8,128)S(1)} %fusion.41) | copy-start | bytes 2308
  142.5 13.0 %copy-start.29 = (f32[6,8,128]{2,1,0:T(8,128)}, f32[6,8,128]{2,1,0:T(8,128)S(1)}, u32[]{:S(2)}) copy-start(f32[6,8,128]{2,1,0:T(8,128)S(1)} %get-tuple-element.228) | copy-start | bytes 73732
  142.5 22.1 %copy-start.33 = (f32[6,8]{1,0:T(8,128)}, f32[6,8]{1,0:T(8,128)S(1)}, u32[]{:S(2)}) copy-start(f32[6,8]{1,0:T(8,128)S(1)} %get-tuple-element.227) | copy-start | bytes 580
  142.7 23.5 %copy-start.49 = (f32[6,8]{1,0:T(8,128)}, f32[6,8]{1,0:T(8,128)S(1)}, u32[]{:S(2)}) copy-start(f32[6,8]{1,0:T(8,128)S(1)} %fusion.88) | copy-start | bytes 580
  145.2 4.8 %copy-start.16 = (bf16[128,6,64]{0,2,1:T(8,128)(2,1)}, bf16[128,6,64]{0,2,1:T(8,128)(2,1)S(1)}, u32[]{:S(2)}) copy-start(bf16[128,6,64]{0,2,1:T(8,128)(2,1)S(1)} %get-tuple-element.231) | copy-start | bytes 294916
  145.5 6.0 %copy-start.64 = (f32[6,128]{1,0:T(8,128)}, f32[6,128]{1,0:T(8,128)S(1)}, u32[]{:S(2)}) copy-start(f32[6,128]{1,0:T(8,128)S(1)} %fusion.39) | copy-start | bytes 9220
  151.5 3.9 %copy-start.28 = (bf16[1,128,384]{2,1,0:T(8,128)(2,1)S(1)}, bf16[1,128,384]{2,1,0:T(8,128)(2,1)}, u32[]{:S(2)}) copy-start(bf16[1,128,384]{2,1,0:T(8,128)(2,1)} %get-tuple-element.210) | copy-start | bytes 294916
  158.4 4.1 %copy-start.76 = (pred[4,6]{0,1:T(8,128)(4,1)S(1)}, pred[4,6]{0,1:T(8,128)(4,1)}, u32[]{:S(2)}) copy-start(pred[4,6]{0,1:T(8,128)(4,1)} %iota_compare_fusion.2) | copy-start | bytes 76
  160.8 4.6 %copy-start.51 = (f32[6,32]{1,0:T(8,128)S(1)}, f32[6,32]{1,0:T(8,128)}, u32[]{:S(2)}) copy-start(f32[6,32]{1,0:T(8,128)} %copy-done.50) | copy-start | bytes 2308
  160.8 6.1 %copy-start.65 = (f32[6,128]{1,0:T(8,128)S(1)}, f32[6,128]{1,0:T(8,128)}, u32[]{:S(2)}) copy-start(f32[6,128]{1,0:T(8,128)} %copy-done.64) | copy-start | bytes 9220
  162.8 18.5 %copy-start.47 = (pred[512,6]{0,1:T(8,128)(4,1)}, pred[512,6]{0,1:T(8,128)(4,1)S(1)}, u32[]{:S(2)}) copy-start(pred[512,6]{0,1:T(8,128)(4,1)S(1)} %broadcast_in_dim.589) | copy-start | bytes 9220
  212.1 6.7 %copy-start.27 = (f32[32,16,6]{1,0,2:T(8,128)S(1)}, f32[32,16,6]{1,0,2:T(8,128)}, u32[]{:S(2)}) copy-start(f32[32,16,6]{1,0,2:T(8,128)} %reshape.821) | copy-start | bytes 36868
  213.9 5.8 %copy-start.30 = (bf16[32,6,64]{2,0,1:T(8,128)(2,1)}, bf16[32,6,64]{2,0,1:T(8,128)(2,1)S(1)}, u32[]{:S(2)}) copy-start(bf16[32,6,64]{2,0,1:T(8,128)(2,1)S(1)} %constant_dynamic-update-slice_fusion.66) | copy-start | bytes 73732
  214.6 5.1 %copy-start.68 = (f32[32,6]{0,1:T(8,128)}, f32[32,6]{0,1:T(8,128)S(1)}, u32[]{:S(2)}) copy-start(f32[32,6]{0,1:T(8,128)S(1)} %stack.83) | copy-start | bytes 2308
  219.8 13.1 %copy-start.14 = (f32[1,128,384]{2,0,1:T(1,128)S(1)}, f32[1,128,384]{2,0,1:T(1,128)}, u32[]{:S(2)}) copy-start(f32[1,128,384]{2,0,1:T(1,128)} %copy.980) | copy-start | bytes 589828
  237.9 3.5 copy-start.11
  249.4 2.9 copy-start.35
  249.5 2.9 copy-start.37
  249.5 2.9 copy-start.39
  249.5 2.9 copy-start.41
  249.5 2.9 copy-start.44
  249.5 2.9 copy-start.46
  263.4 3.7 %copy-start.13 = (bf16[1,128,384]{1,2,0:T(8,128)(2,1)S(1)}, bf16[1,128,384]{1,2,0:T(8,128)(2,1)}, u32[]{:S(2)}) copy-start(bf16[1,128,384]{1,2,0:T(8,128)(2,1)} %copy-done.12) | copy-start | bytes 294916
  263.4 3.7 %copy-start.63 = (bf16[6,8,128]{2,1,0:T(8,128)(2,1)S(1)}, bf16[6,8,128]{2,1,0:T(8,128)(2,1)}, u32[]{:S(2)}) copy-start(bf16[6,8,128]{2,1,0:T(8,128)(2,1)} %copy-done.62) | copy-start | bytes 36868
  (31 other events, 49.4 us)
Sparse Core Ops, SparseCore 0:
  238.1 97.1 all-reduce.4
where the time goes:
time: 368 us; the launch traced here: 362 us
  local copies, waits for them, and re-layouts  179 us (49%)
  blocking collectives  70.4 us (19%)
  waiting for transfers between devices  60 us (16%)
  other arithmetic  23.9 us (6%)
  between operations  17.1 us (5%)
  matrix products  12.4 us (3%)
    broadcast_in_dim x74, local copies, waits for them, and re-layouts, spread(): placed = jnp.where(selector, matrix[:, None], filler)  60.9 us
    unnamed x2, waiting for transfers between devices  60 us
    all_gather x1, blocking collectives, shards(): lax.all_gather(far_pair, ('outer', 'inner'), axis=1, tiled=True)  40.7 us
    unnamed x256, local copies, waits for them, and re-layouts  34.4 us
    slice x30, local copies, waits for them, and re-layouts, pick(): folded[:, head % stride, head]  31.2 us
    all_gather x1, blocking collectives, shards(): lax.all_gather(mid_pair, ('outer', 'inner'), axis=1, tiled=True)  29.7 us
    another operation x12, local copies, waits for them, and re-layouts, pick(): folded = matrix.reshape((length // stride, stride) + matrix.shape[1:])  18.3 us
    another operation x2, local copies, waits for them, and re-layouts, shards(): jnp.stack([gk_far.reshape(-1, width), gv_far.reshape(-1, width)])  13.3 us
  transfers between devices with their start and end apart: 1, of which 1 were waited for; matrix products, arithmetic and copies ran while one was open for 10% of the time, Pallas kernels for 0%

commit v1 on v0

--- a/solution.py
+++ b/solution.py
@@ -1,6 +1,10 @@
+import functools
+
 import jax
 import jax.numpy as jnp
 from jax import lax
+from jax.experimental import pallas as pl
+from jax.experimental.pallas import tpu as pltpu
 from jax.sharding import PartitionSpec as P
 
 E = 64
@@ -65,7 +69,7 @@
     return part_grads(*items)
 
 
-def shards(queries, key_rows, value_rows, grad_out):
+def general_shards(queries, key_rows, value_rows, grad_out):
     rows = queries.shape[0]
     width = queries.shape[1]
     heads = width // E
@@ -200,6 +204,278 @@
     )
 
 
+def dot_nt(left, right):
+    return lax.dot_general(left, right, (((1,), (1,)), ((), ())), preferred_element_type=jnp.float32)
+
+
+def dot_nn(left, right):
+    return lax.dot_general(left, right, (((1,), (0,)), ((), ())), preferred_element_type=jnp.float32)
+
+
+def dot_tn(left, right):
+    return lax.dot_general(left, right, (((0,), (0,)), ((), ())), preferred_element_type=jnp.float32)
+
+
+def chunk_offsets(head, stride):
+    first = head % stride
+    return [first] + [t for t in range(head % R1, stride, R1) if t != first]
+
+
+def slide_kernel(
+    devices, inner, heads, stride,
+    q_ref, k_ref, v_ref, g_ref,
+    out_ref, gq_ref, gk_ref, gv_ref,
+    qf, kf, vf, gf, qg_near, kv_near, kv_far, part, recv,
+    send_a, recv_a, send_b, recv_b,
+):
+    rows = q_ref.shape[0]
+    far = rows // stride
+    near = rows // R1
+    pairs = heads // 2
+    scale = E ** (-0.5)
+    outer_id = lax.axis_index("outer")
+    inner_id = lax.axis_index("inner")
+    me = outer_id * inner + inner_id
+
+    def target(peer):
+        return {"outer": peer // inner, "inner": lax.rem(peer, inner)}
+
+    def peer_of(step):
+        return lax.rem(me + step, devices)
+
+    barrier = pltpu.get_barrier_semaphore()
+
+    def greet(step, carry):
+        pl.semaphore_signal(
+            barrier, inc=1, device_id=target(peer_of(step)), device_id_type=pl.DeviceIdType.MESH
+        )
+        return carry
+
+    lax.fori_loop(1, devices, greet, 0)
+
+    lane = lax.broadcasted_iota(jnp.int32, (far, 2 * E), 1)
+    low = lane < E
+
+    def swap(x):
+        return pltpu.roll(x, E, 1)
+
+    def joined(left_f, right_f, head, offset):
+        a = left_f[head // 2, pl.ds(offset, far, stride=stride), :]
+        b = right_f[head // 2, pl.ds(offset, far, stride=stride), :]
+        if head % 2 == 0:
+            return jnp.where(low, a, swap(b)).astype(jnp.bfloat16)
+        return jnp.where(low, swap(a), b).astype(jnp.bfloat16)
+
+    def widen(wide, ref):
+        for pair in range(pairs):
+            wide[pair] = ref[:, pl.ds(pair * 2 * E, 2 * E)].astype(jnp.float32)
+
+    def narrow(ref, wide):
+        for pair in range(pairs):
+            ref[:, pl.ds(pair * 2 * E, 2 * E)] = wide[pair].astype(jnp.bfloat16)
+
+    widen(kf, k_ref)
+    widen(vf, v_ref)
+    for head in range(heads):
+        block = joined(kf, vf, head, chunk_offsets(head, stride)[0])
+        kv_near[head, pl.ds(0, far), :] = block
+        kv_far[me, head, :, :] = block
+
+    pl.semaphore_wait(barrier, devices - 1)
+
+    def gather_copy(step):
+        peer = peer_of(step)
+        return pltpu.make_async_remote_copy(
+            src_ref=kv_far.at[me],
+            dst_ref=kv_far.at[me],
+            send_sem=send_a.at[step],
+            recv_sem=recv_a.at[me],
+            device_id=target(peer),
+            device_id_type=pl.DeviceIdType.MESH,
+        )
+
+    def gather_arrival(step):
+        peer = peer_of(step)
+        return pltpu.make_async_remote_copy(
+            src_ref=kv_far.at[peer],
+            dst_ref=kv_far.at[peer],
+            send_sem=send_a.at[step],
+            recv_sem=recv_a.at[peer],
+            device_id=target(peer),
+            device_id_type=pl.DeviceIdType.MESH,
+        )
+
+    def run(fn):
+        def body(step, carry):
+            fn(step)
+            return carry
+        lax.fori_loop(1, devices, body, 0)
+
+    run(lambda step: gather_copy(step).start())
+
+    widen(qf, q_ref)
+    widen(gf, g_ref)
+    for head in range(heads):
+        for index, offset in enumerate(chunk_offsets(head, stride)):
+            span = pl.ds(index * far, far)
+            if index:
+                kv_near[head, span, :] = joined(kf, vf, head, offset)
+            qg_near[head, span, :] = joined(qf, gf, head, offset)
+
+    zeros = jnp.zeros((far, 2 * E), jnp.float32)
+    for ref in (qf, kf, vf, gf):
+        for pair in range(pairs):
+            for offset in range(stride):
+                if offset % R1 not in ((2 * pair) % R1, (2 * pair + 1) % R1):
+                    ref[pair, pl.ds(offset, far, stride=stride), :] = zeros
+
+    def split(qg):
+        half = lax.broadcasted_iota(jnp.int32, qg.shape, 1) < E
+        none = jnp.zeros_like(qg)
+        return jnp.where(half, qg, none), jnp.where(half, none, qg)
+
+    def attend(q_only, g_only, score_keys, counts):
+        scores = jnp.concatenate([dot_nt(q_only, keys) for keys in score_keys], axis=1) * scale
+        grad_w = jnp.concatenate([dot_nt(g_only, keys) for keys in score_keys], axis=1)
+        peak = jnp.max(scores, axis=1, keepdims=True)
+        weights = jnp.exp(scores - peak)
+        if counts is not None:
+            weights = weights * counts
+        mass = jnp.sum(weights, axis=1, keepdims=True)
+        inverse = 1.0 / mass
+        rounded = weights.astype(jnp.bfloat16)
+        summed, start = None, 0
+        for keys in score_keys:
+            term = dot_nn(rounded[:, start:start + keys.shape[0]], keys)
+            summed = term if summed is None else summed + term
+            start += keys.shape[0]
+        result = summed * inverse
+        dots = jnp.sum(g_only.astype(jnp.float32) * result, axis=1, keepdims=True)
+        shares = weights * inverse
+        grad_s = (shares * (grad_w - dots) * scale).astype(jnp.bfloat16)
+        grad_q, start = None, 0
+        for keys in score_keys:
+            term = dot_nn(grad_s[:, start:start + keys.shape[0]], keys)
+            grad_q = term if grad_q is None else grad_q + term
+            start += keys.shape[0]
+        both = jnp.concatenate([grad_s, shares.astype(jnp.bfloat16)], axis=0)
+        grad_kv = dot_tn(both, jnp.concatenate([q_only, g_only], axis=0))
+        return result, grad_q, grad_kv
+
+    def place(ref, head, index, value, high):
+        offset = chunk_offsets(head, stride)[index]
+        odd = head % 2 == 1
+        if odd != high:
+            value = swap(value)
+        kept = jnp.where(low, 0.0, value) if odd else jnp.where(low, value, 0.0)
+        ref[head // 2, pl.ds(offset, far, stride=stride), :] = kept
+
+    near_grads = []
+    for head in range(heads):
+        keys = kv_near[head]
+        q_only, g_only = split(qg_near[head, pl.ds(far, near - far), :])
+        result, grad_q, grad_kv = attend(q_only, g_only, [keys], None)
+        for index in range(1, stride // R1):
+            rows_in = slice((index - 1) * far, index * far)
+            place(vf, head, index, result[rows_in], True)
+            place(qf, head, index, grad_q[rows_in], False)
+        near_grads.append(grad_kv)
+
+    run(lambda step: gather_arrival(step).wait_recv())
+
+    total = devices * far
+    row_id = lax.broadcasted_iota(jnp.int32, (far, near + total), 0)
+    col_id = lax.broadcasted_iota(jnp.int32, (far, near + total), 1)
+    ratio = R2 // stride
+    twice = (col_id >= near) & (row_id % ratio == 0) & ((col_id - near) % ratio == 0)
+    counts = jnp.where(twice, 2.0, 1.0)
+    for head in range(heads):
+        keys = kv_near[head]
+        far_keys = kv_far[:, head].reshape(total, 2 * E)
+        q_only, g_only = split(qg_near[head, pl.ds(0, far), :])
+        result, grad_q, grad_kv = attend(q_only, g_only, [keys, far_keys], counts)
+        place(vf, head, 0, result, True)
+        place(qf, head, 0, grad_q, False)
+        near_grads[head] = near_grads[head] + grad_kv[:near]
+        part[:, head] = grad_kv[near:].reshape(devices, far, 2 * E).astype(jnp.bfloat16)
+    recv[me] = part[me]
+
+    def scatter_copy(step):
+        peer = peer_of(step)
+        return pltpu.make_async_remote_copy(
+            src_ref=part.at[peer],
+            dst_ref=recv.at[me],
+            send_sem=send_b.at[step],
+            recv_sem=recv_b.at[me],
+            device_id=target(peer),
+            device_id_type=pl.DeviceIdType.MESH,
+        )
+
+    def scatter_arrival(step):
+        peer = peer_of(step)
+        return pltpu.make_async_remote_copy(
+            src_ref=part.at[peer],
+            dst_ref=recv.at[peer],
+            send_sem=send_b.at[step],
+            recv_sem=recv_b.at[peer],
+            device_id=target(peer),
+            device_id_type=pl.DeviceIdType.MESH,
+        )
+
+    run(lambda step: scatter_copy(step).start())
+    narrow(out_ref, vf)
+    narrow(gq_ref, qf)
+    for head in range(heads):
+        for index in range(1, stride // R1):
+            piece = near_grads[head][index * far:(index + 1) * far]
+            place(kf, head, index, piece, False)
+            place(gf, head, index, piece, True)
+    run(lambda step: scatter_arrival(step).wait_recv())
+    for head in range(heads):
+        piece = near_grads[head][:far] + jnp.sum(recv[:, head].astype(jnp.float32), axis=0)
+        place(kf, head, 0, piece, False)
+        place(gf, head, 0, piece, True)
+    narrow(gk_ref, kf)
+    narrow(gv_ref, gf)
+    run(lambda step: gather_copy(step).wait_send())
+    run(lambda step: scatter_copy(step).wait_send())
+
+
+def slide_shards(queries, key_rows, value_rows, grad_out):
+    rows, width = queries.shape
+    heads = width // E
+    inner = lax.axis_size("inner")
+    devices = lax.axis_size("outer") * inner
+    stride = rows * devices // KEYS
+    far = rows // stride
+    near = rows // R1
+    whole = pl.BlockSpec(memory_space=pltpu.VMEM)
+    return pl.pallas_call(
+        functools.partial(slide_kernel, devices, inner, heads, stride),
+        out_shape=[jax.ShapeDtypeStruct((rows, width), jnp.bfloat16)] * 4,
+        in_specs=[whole] * 4,
+        out_specs=[whole] * 4,
+        scratch_shapes=[pltpu.VMEM((heads // 2, rows, 2 * E), jnp.float32)] * 4
+        + [pltpu.VMEM((heads, near, 2 * E), jnp.bfloat16)] * 2
+        + [pltpu.VMEM((devices, heads, far, 2 * E), jnp.bfloat16)] * 3
+        + [pltpu.SemaphoreType.DMA((devices,))] * 4,
+        compiler_params=pltpu.CompilerParams(
+            collective_id=0, has_side_effects=True, vmem_limit_bytes=48 * 1024 * 1024
+        ),
+    )(queries, key_rows, value_rows, grad_out)
+
+
+def shards(queries, key_rows, value_rows, grad_out):
+    rows, width = queries.shape
+    devices = lax.axis_size("outer") * lax.axis_size("inner")
+    stride = rows * devices // KEYS
+    one_segment = rows * devices == W2 and rows == W1 and (width // E) % 2 == 0
+    nested = stride % R1 == 0 and R2 % stride == 0 and rows % (16 * stride) == 0
+    if one_segment and nested and width // E <= stride:
+        return slide_shards(queries, key_rows, value_rows, grad_out)
+    return general_shards(queries, key_rows, value_rows, grad_out)
+
+
 def solution(mesh):
     return jax.shard_map(
         shards,

time: 368 us -> 53.1 us (0.14)
  the two profiles are of different devices: /device:TPU:0 before, /device:TPU:29 now
where the time goes in v1:
time: 53.1 us; the launch traced here: 52.8 us
  Pallas kernels  45.2 us (85%)
  local copies, waits for them, and re-layouts  6.96 us (13%)
  between operations  0.65 us (1%)
    pallas_call x1, Pallas kernels, slide_shards(): pl.pallas_call(functools.partial(slide_kernel, devices, inner, heads, str...  45.2 us
    unnamed x12, local copies, waits for them, and re-layouts  6.96 us

profile of v1, /device:TPU:29, one launch (start us, length us, event | category | flops | bytes accessed | tf_op | source)
XLA Modules:
  0.0 52.8 jit_solution(7126179037365583746)
XLA Ops:
  0.6 0.0 copy-start
  0.6 1.0 %copy-done = bf16[512,384]{1,0:T(8,128)(2,1)S(1)} copy-done((bf16[512,384]{1,0:T(8,128)(2,1)S(1)}, bf16[512,384]{1,0:T(8,128)(2,1)}, u32[]{:S(2)}) %copy-start) | copy-done | bytes 393240
  1.6 0.0 copy-start.1
  1.6 1.0 %copy-done.1 = bf16[512,384]{1,0:T(8,128)(2,1)S(1)} copy-done((bf16[512,384]{1,0:T(8,128)(2,1)S(1)}, bf16[512,384]{1,0:T(8,128)(2,1)}, u32[]{:S(2)}) %copy-start.1) | copy-done | bytes 393240
  2.6 0.0 copy-start.2
  2.6 1.0 %copy-done.2 = bf16[512,384]{1,0:T(8,128)(2,1)S(1)} copy-done((bf16[512,384]{1,0:T(8,128)(2,1)S(1)}, bf16[512,384]{1,0:T(8,128)(2,1)}, u32[]{:S(2)}) %copy-start.2) | copy-done | bytes 393240
  3.6 0.0 copy-start.3
  3.6 1.0 %copy-done.3 = bf16[512,384]{1,0:T(8,128)(2,1)S(1)} copy-done((bf16[512,384]{1,0:T(8,128)(2,1)S(1)}, bf16[512,384]{1,0:T(8,128)(2,1)}, u32[]{:S(2)}) %copy-start.3) | copy-done | bytes 393240
  4.6 45.2 %shard_map.75 = (bf16[512,384]{1,0:T(8,128)(2,1)S(1)}, bf16[512,384]{1,0:T(8,128)(2,1)S(1)}, bf16[512,384]{1,0:T(8,128)(2,1)S(1)}, bf16[512,384]{1,0:T(8,128)(2,1)S(1)}) custom-call(bf16[512,384]{1,0:T(8,128)(2,1)S(1)} %copy-done, bf16[512,384]{1,0:T(8,128)(2,1)S(1)} %copy-done.1, bf16[512,384]{1,0:T(8,128)(2,1)S(1)} %copy-done.2, bf16[512,384]{1,0:T(8,128)(2,1)S(1)} %copy-done.3), custom_call_target="tpu_custom_call" | custom-call | tf_op jit(solution)/shard_map/pallas_call | solution.py:453
  49.8 0.7 %copy.12 = bf16[512,384]{1,0:T(8,128)(2,1)} copy(bf16[512,384]{1,0:T(8,128)(2,1)S(1)} %get-tuple-element.8) | data formatting | bytes 786432
  50.5 0.7 %copy.13 = bf16[512,384]{1,0:T(8,128)(2,1)} copy(bf16[512,384]{1,0:T(8,128)(2,1)S(1)} %get-tuple-element.9) | data formatting | bytes 786432
  51.3 0.7 %copy.14 = bf16[512,384]{1,0:T(8,128)(2,1)} copy(bf16[512,384]{1,0:T(8,128)(2,1)S(1)} %get-tuple-element.10) | data formatting | bytes 786432
  52.0 0.7 %copy.15 = bf16[512,384]{1,0:T(8,128)(2,1)} copy(bf16[512,384]{1,0:T(8,128)(2,1)S(1)} %get-tuple-element.11) | data formatting | bytes 786432
Async XLA Ops:
  0.6 1.0 %copy-start = (bf16[512,384]{1,0:T(8,128)(2,1)S(1)}, bf16[512,384]{1,0:T(8,128)(2,1)}, u32[]{:S(2)}) copy-start(bf16[512,384]{1,0:T(8,128)(2,1)} %q_ref.1) | copy-start | bytes 1179652
  1.6 1.0 %copy-start.1 = (bf16[512,384]{1,0:T(8,128)(2,1)S(1)}, bf16[512,384]{1,0:T(8,128)(2,1)}, u32[]{:S(2)}) copy-start(bf16[512,384]{1,0:T(8,128)(2,1)} %k_ref.1) | copy-start | bytes 1179652
  2.6 1.0 %copy-start.2 = (bf16[512,384]{1,0:T(8,128)(2,1)S(1)}, bf16[512,384]{1,0:T(8,128)(2,1)}, u32[]{:S(2)}) copy-start(bf16[512,384]{1,0:T(8,128)(2,1)} %v_ref.1) | copy-start | bytes 1179652
  3.6 1.0 %copy-start.3 = (bf16[512,384]{1,0:T(8,128)(2,1)S(1)}, bf16[512,384]{1,0:T(8,128)(2,1)}, u32[]{:S(2)}) copy-start(bf16[512,384]{1,0:T(8,128)(2,1)} %g_ref.1) | copy-start | bytes 1179652

commit v2 on v1

--- a/solution.py
+++ b/solution.py
@@ -222,12 +222,25 @@
 
 
 def slide_kernel(
-    devices, inner, heads, stride,
-    q_ref, k_ref, v_ref, g_ref,
+    inner, heads, stride,
+    q_hbm, k_hbm, v_hbm, g_hbm,
     out_ref, gq_ref, gk_ref, gv_ref,
-    qf, kf, vf, gf, qg_near, kv_near, kv_far, part, recv,
-    send_a, recv_a, send_b, recv_b,
+    q_ref, k_ref, v_ref, g_ref, load_sem,
+    qf, kf, vf, gf, qg_near, kv_near, kv_far, part, from_core, by_x, from_x, by_z, from_z,
+    send_a, recv_a, send_core, recv_core, send_x, recv_x, send_z, recv_z,
 ):
+    loads = [
+        pltpu.make_async_copy(source, target, load_sem.at[index])
+        for index, (source, target) in enumerate(
+            ((k_hbm, k_ref), (v_hbm, v_ref), (q_hbm, q_ref), (g_hbm, g_ref))
+        )
+    ]
+    for load in loads:
+        load.start()
+    devices = 2 * inner
+    zs = inner // 2
+    groups = kv_far.shape[0]
+    group_heads = heads // groups
     rows = q_ref.shape[0]
     far = rows // stride
     near = rows // R1
@@ -236,22 +249,22 @@
     outer_id = lax.axis_index("outer")
     inner_id = lax.axis_index("inner")
     me = outer_id * inner + inner_id
-
-    def target(peer):
-        return {"outer": peer // inner, "inner": lax.rem(peer, inner)}
-
-    def peer_of(step):
-        return lax.rem(me + step, devices)
-
+    my_z = inner_id // 2
+    my_x = lax.rem(inner_id, 2)
+    MESH = pl.DeviceIdType.MESH
+    to_core = {"outer": 1 - outer_id, "inner": inner_id}
+    to_x = {"outer": outer_id, "inner": 2 * my_z + 1 - my_x}
+
+    def peer_z(step):
+        return lax.rem(my_z + step, zs)
+
+    def to_z(step):
+        return {"outer": outer_id, "inner": 2 * peer_z(step) + my_x}
+
+    neighbours = [to_core, to_x] + [to_z(step) for step in range(1, zs)]
     barrier = pltpu.get_barrier_semaphore()
-
-    def greet(step, carry):
-        pl.semaphore_signal(
-            barrier, inc=1, device_id=target(peer_of(step)), device_id_type=pl.DeviceIdType.MESH
-        )
-        return carry
-
-    lax.fori_loop(1, devices, greet, 0)
+    for neighbour in neighbours:
+        pl.semaphore_signal(barrier, inc=1, device_id=neighbour, device_id_type=MESH)
 
     lane = lax.broadcasted_iota(jnp.int32, (far, 2 * E), 1)
     low = lane < E
@@ -274,46 +287,74 @@
         for pair in range(pairs):
             ref[:, pl.ds(pair * 2 * E, 2 * E)] = wide[pair].astype(jnp.bfloat16)
 
+    loads[0].wait()
     widen(kf, k_ref)
+    loads[1].wait()
     widen(vf, v_ref)
     for head in range(heads):
         block = joined(kf, vf, head, chunk_offsets(head, stride)[0])
         kv_near[head, pl.ds(0, far), :] = block
-        kv_far[me, head, :, :] = block
-
-    pl.semaphore_wait(barrier, devices - 1)
-
-    def gather_copy(step):
-        peer = peer_of(step)
-        return pltpu.make_async_remote_copy(
-            src_ref=kv_far.at[me],
-            dst_ref=kv_far.at[me],
-            send_sem=send_a.at[step],
-            recv_sem=recv_a.at[me],
-            device_id=target(peer),
-            device_id_type=pl.DeviceIdType.MESH,
+        kv_far[head // group_heads, me, head % group_heads] = block
+
+    pl.semaphore_wait(barrier, len(neighbours))
+
+    def block_id(core, z, x):
+        return core * inner + 2 * z + x
+
+    pending = []
+
+    def send_block(group, block, slot, device):
+        copy = pltpu.make_async_remote_copy(
+            src_ref=kv_far.at[group, block],
+            dst_ref=kv_far.at[group, block],
+            send_sem=send_a.at[group, slot],
+            recv_sem=recv_a.at[group, block],
+            device_id=device,
+            device_id_type=MESH,
         )
-
-    def gather_arrival(step):
-        peer = peer_of(step)
-        return pltpu.make_async_remote_copy(
-            src_ref=kv_far.at[peer],
-            dst_ref=kv_far.at[peer],
-            send_sem=send_a.at[step],
-            recv_sem=recv_a.at[peer],
-            device_id=target(peer),
-            device_id_type=pl.DeviceIdType.MESH,
-        )
-
-    def run(fn):
-        def body(step, carry):
-            fn(step)
-            return carry
-        lax.fori_loop(1, devices, body, 0)
-
-    run(lambda step: gather_copy(step).start())
-
+        copy.start()
+        pending.append(copy)
+
+    def await_block(group, block):
+        pltpu.make_async_remote_copy(
+            src_ref=kv_far.at[group, block],
+            dst_ref=kv_far.at[group, block],
+            send_sem=send_a.at[group, 0],
+            recv_sem=recv_a.at[group, block],
+            device_id=to_core,
+            device_id_type=MESH,
+        ).wait_recv()
+
+    def send_own(group):
+        for step in range(1, zs):
+            send_block(group, me, step, to_z(step))
+        send_block(group, me, zs, to_x)
+        send_block(group, me, zs + 1, to_core)
+
+    def pass_z(group):
+        for step in range(1, zs):
+            block = block_id(outer_id, peer_z(step), my_x)
+            await_block(group, block)
+            send_block(group, block, zs + 2 * step, to_x)
+            send_block(group, block, zs + 2 * step + 1, to_core)
+
+    def pass_x(group):
+        for step in range(zs):
+            block = block_id(outer_id, peer_z(step), 1 - my_x)
+            await_block(group, block)
+            send_block(group, block, 3 * zs + step, to_core)
+
+    def finish_gather(group):
+        for step in range(zs):
+            for x in (my_x, 1 - my_x):
+                await_block(group, block_id(1 - outer_id, peer_z(step), x))
+
+    for group in range(groups):
+        send_own(group)
+
+    loads[2].wait()
     widen(qf, q_ref)
+    loads[3].wait()
     widen(gf, g_ref)
     for head in range(heads):
         for index, offset in enumerate(chunk_offsets(head, stride)):
@@ -371,7 +412,11 @@
         ref[head // 2, pl.ds(offset, far, stride=stride), :] = kept
 
     near_grads = []
+    handing = [(pass_z, group) for group in range(groups)] + [(pass_x, group) for group in range(groups)]
     for head in range(heads):
+        while len(handing) * heads > 2 * groups * (heads - 1 - head):
+            step, group = handing.pop(0)
+            step(group)
         keys = kv_near[head]
         q_only, g_only = split(qg_near[head, pl.ds(far, near - far), :])
         result, grad_q, grad_kv = attend(q_only, g_only, [keys], None)
@@ -381,86 +426,144 @@
             place(qf, head, index, grad_q[rows_in], False)
         near_grads.append(grad_kv)
 
-    run(lambda step: gather_arrival(step).wait_recv())
-
     total = devices * far
     row_id = lax.broadcasted_iota(jnp.int32, (far, near + total), 0)
     col_id = lax.broadcasted_iota(jnp.int32, (far, near + total), 1)
     ratio = R2 // stride
     twice = (col_id >= near) & (row_id % ratio == 0) & ((col_id - near) % ratio == 0)
     counts = jnp.where(twice, 2.0, 1.0)
+
+    def core_copy(head):
+        return pltpu.make_async_remote_copy(
+            src_ref=part.at[head, 1 - outer_id],
+            dst_ref=from_core.at[head],
+            send_sem=send_core.at[head],
+            recv_sem=recv_core.at[head],
+            device_id=to_core,
+            device_id_type=MESH,
+        )
+
+    def x_copy(head):
+        return pltpu.make_async_remote_copy(
+            src_ref=by_x.at[head, 1 - my_x],
+            dst_ref=from_x.at[head],
+            send_sem=send_x.at[head],
+            recv_sem=recv_x.at[head],
+            device_id=to_x,
+            device_id_type=MESH,
+        )
+
+    def z_copy(head, step, slot):
+        return pltpu.make_async_remote_copy(
+            src_ref=by_z.at[head, peer_z(step)],
+            dst_ref=from_z.at[head, slot],
+            send_sem=send_z.at[head, step],
+            recv_sem=recv_z.at[head, slot],
+            device_id=to_z(step),
+            device_id_type=MESH,
+        )
+
+    def reduce_core(head):
+        core_copy(head).wait_recv()
+        both = part[head, outer_id].astype(jnp.float32) + from_core[head].astype(jnp.float32)
+        both = both.astype(jnp.bfloat16).reshape(zs, 2, far, 2 * E)
+        for x in range(2):
+            by_x[head, x] = both[:, x]
+        x_copy(head).start()
+
+    def reduce_x(head):
+        x_copy(head).wait_recv()
+        both = by_x[head, my_x].astype(jnp.float32) + from_x[head].astype(jnp.float32)
+        by_z[head] = both.astype(jnp.bfloat16)
+        for step in range(1, zs):
+            z_copy(head, step, my_z).start()
+
     for head in range(heads):
+        if head % group_heads == 0:
+            finish_gather(head // group_heads)
         keys = kv_near[head]
-        far_keys = kv_far[:, head].reshape(total, 2 * E)
+        far_keys = kv_far[head // group_heads, :, head % group_heads].reshape(total, 2 * E)
         q_only, g_only = split(qg_near[head, pl.ds(0, far), :])
         result, grad_q, grad_kv = attend(q_only, g_only, [keys, far_keys], counts)
         place(vf, head, 0, result, True)
         place(qf, head, 0, grad_q, False)
         near_grads[head] = near_grads[head] + grad_kv[:near]
-        part[:, head] = grad_kv[near:].reshape(devices, far, 2 * E).astype(jnp.bfloat16)
-    recv[me] = part[me]
-
-    def scatter_copy(step):
-        peer = peer_of(step)
-        return pltpu.make_async_remote_copy(
-            src_ref=part.at[peer],
-            dst_ref=recv.at[me],
-            send_sem=send_b.at[step],
-            recv_sem=recv_b.at[me],
-            device_id=target(peer),
-            device_id_type=pl.DeviceIdType.MESH,
-        )
-
-    def scatter_arrival(step):
-        peer = peer_of(step)
-        return pltpu.make_async_remote_copy(
-            src_ref=part.at[peer],
-            dst_ref=recv.at[peer],
-            send_sem=send_b.at[step],
-            recv_sem=recv_b.at[peer],
-            device_id=target(peer),
-            device_id_type=pl.DeviceIdType.MESH,
-        )
-
-    run(lambda step: scatter_copy(step).start())
+        part[head] = grad_kv[near:].reshape(2, inner, far, 2 * E).astype(jnp.bfloat16)
+        core_copy(head).start()
+        if head >= 1:
+            reduce_core(head - 1)
+        if head >= 2:
+            reduce_x(head - 2)
+
+    reduce_core(heads - 1)
+    reduce_x(heads - 2)
     narrow(out_ref, vf)
+    reduce_x(heads - 1)
     narrow(gq_ref, qf)
     for head in range(heads):
         for index in range(1, stride // R1):
             piece = near_grads[head][index * far:(index + 1) * far]
             place(kf, head, index, piece, False)
             place(gf, head, index, piece, True)
-    run(lambda step: scatter_arrival(step).wait_recv())
     for head in range(heads):
-        piece = near_grads[head][:far] + jnp.sum(recv[:, head].astype(jnp.float32), axis=0)
+        piece = near_grads[head][:far] + by_z[head, my_z].astype(jnp.float32)
+        for step in range(1, zs):
+            z_copy(head, step, peer_z(step)).wait_recv()
+            piece = piece + from_z[head, peer_z(step)].astype(jnp.float32)
         place(kf, head, 0, piece, False)
         place(gf, head, 0, piece, True)
     narrow(gk_ref, kf)
     narrow(gv_ref, gf)
-    run(lambda step: gather_copy(step).wait_send())
-    run(lambda step: scatter_copy(step).wait_send())
+    for copy in pending:
+        copy.wait_send()
+    for head in range(heads):
+        core_copy(head).wait_send()
+        x_copy(head).wait_send()
+        for step in range(1, zs):
+            z_copy(head, step, my_z).wait_send()
 
 
 def slide_shards(queries, key_rows, value_rows, grad_out):
     rows, width = queries.shape
     heads = width // E
     inner = lax.axis_size("inner")
-    devices = lax.axis_size("outer") * inner
+    devices = 2 * inner
+    zs = inner // 2
     stride = rows * devices // KEYS
     far = rows // stride
     near = rows // R1
+    groups = 2
+    bf16 = jnp.bfloat16
     whole = pl.BlockSpec(memory_space=pltpu.VMEM)
+    dma = pltpu.SemaphoreType.DMA
     return pl.pallas_call(
-        functools.partial(slide_kernel, devices, inner, heads, stride),
-        out_shape=[jax.ShapeDtypeStruct((rows, width), jnp.bfloat16)] * 4,
-        in_specs=[whole] * 4,
+        functools.partial(slide_kernel, inner, heads, stride),
+        out_shape=[jax.ShapeDtypeStruct((rows, width), bf16)] * 4,
+        in_specs=[pl.BlockSpec(memory_space=pltpu.HBM)] * 4,
         out_specs=[whole] * 4,
-        scratch_shapes=[pltpu.VMEM((heads // 2, rows, 2 * E), jnp.float32)] * 4
-        + [pltpu.VMEM((heads, near, 2 * E), jnp.bfloat16)] * 2
-        + [pltpu.VMEM((devices, heads, far, 2 * E), jnp.bfloat16)] * 3
-        + [pltpu.SemaphoreType.DMA((devices,))] * 4,
+        scratch_shapes=[pltpu.VMEM((rows, width), bf16)] * 4
+        + [dma((4,))]
+        + [pltpu.VMEM((heads // 2, rows, 2 * E), jnp.float32)] * 4
+        + [pltpu.VMEM((heads, near, 2 * E), bf16)] * 2
+        + [
+            pltpu.VMEM((groups, devices, heads // groups, far, 2 * E), bf16),
+            pltpu.VMEM((heads, 2, inner, far, 2 * E), bf16),
+            pltpu.VMEM((heads, inner, far, 2 * E), bf16),
+            pltpu.VMEM((heads, 2, zs, far, 2 * E), bf16),
+            pltpu.VMEM((heads, zs, far, 2 * E), bf16),
+            pltpu.VMEM((heads, zs, far, 2 * E), bf16),
+            pltpu.VMEM((heads, zs, far, 2 * E), bf16),
+            dma((groups, 4 * zs)),
+            dma((groups, devices)),
+            dma((heads,)),
+            dma((heads,)),
+            dma((heads,)),
+            dma((heads,)),
+            dma((heads, zs)),
+            dma((heads, zs)),
+        ],
         compiler_params=pltpu.CompilerParams(
-            collective_id=0, has_side_effects=True, vmem_limit_bytes=48 * 1024 * 1024
+            collective_id=0, has_side_effects=True, vmem_limit_bytes=63 * 1024 * 1024
         ),
     )(queries, key_rows, value_rows, grad_out)
 
@@ -471,7 +574,8 @@
     stride = rows * devices // KEYS
     one_segment = rows * devices == W2 and rows == W1 and (width // E) % 2 == 0
     nested = stride % R1 == 0 and R2 % stride == 0 and rows % (16 * stride) == 0
-    if one_segment and nested and width // E <= stride:
+    paired = lax.axis_size("outer") == 2 and lax.axis_size("inner") % 2 == 0
+    if one_segment and nested and paired and width // E <= stride:
         return slide_shards(queries, key_rows, value_rows, grad_out)
     return general_shards(queries, key_rows, value_rows, grad_out)
 

time: 53.1 us -> 39.4 us (0.74)
  the two profiles are of different devices: /device:TPU:29 before, /device:TPU:0 now
where the time goes in v2:
time: 39.4 us; the launch traced here: 39.1 us
  Pallas kernels  33.6 us (85%)
  local copies, waits for them, and re-layouts  4.85 us (12%)
  between operations  0.65 us (2%)
    pallas_call x1, Pallas kernels, slide_shards(): pl.pallas_call(functools.partial(slide_kernel, inner, heads, stride), out...  33.6 us
    unnamed x10, local copies, waits for them, and re-layouts  4.85 us

profile of v2, /device:TPU:0, one launch (start us, length us, event | category | flops | bytes accessed | tf_op | source)
XLA Modules:
  0.0 39.1 jit_solution(127698466199201109)
XLA Ops:
  0.6 33.6 %shard_map.75 = (bf16[512,384]{1,0:T(8,128)(2,1)}, bf16[512,384]{1,0:T(8,128)(2,1)}, bf16[512,384]{1,0:T(8,128)(2,1)}, bf16[512,384]{1,0:T(8,128)(2,1)}) custom-call(bf16[512,384]{1,0:T(8,128)(2,1)} %q_hbm.1, bf16[512,384]{1,0:T(8,128)(2,1)} %k_hbm.1, bf16[512,384]{1,0:T(8,128)(2,1)} %v_hbm.1, bf16[512,384]{1,0:T(8,128)(2,1)} %g_hbm.1), custom_call_target="tpu_custom_call" | custom-call | tf_op jit(solution)/shard_map/pallas_call | solution.py:539
  34.3 0.0 copy-start.2
  34.3 1.8 %copy.12 = bf16[512,384]{1,0:T(8,128)(2,1)} copy(bf16[512,384]{1,0:T(8,128)(2,1)} %get-tuple-element.8) | data formatting | bytes 786432
  36.1 0.0 copy-done.2
  36.1 0.0 copy-start.1
  36.1 0.7 %copy.13 = bf16[512,384]{1,0:T(8,128)(2,1)} copy(bf16[512,384]{1,0:T(8,128)(2,1)S(1)} %copy-done.2) | data formatting | bytes 786432
  36.9 0.4 copy-done.1
  37.3 0.0 copy-start
  37.3 0.7 %copy.14 = bf16[512,384]{1,0:T(8,128)(2,1)} copy(bf16[512,384]{1,0:T(8,128)(2,1)S(1)} %copy-done.1) | data formatting | bytes 786432
  38.0 0.4 copy-done
  38.4 0.7 %copy.15 = bf16[512,384]{1,0:T(8,128)(2,1)} copy(bf16[512,384]{1,0:T(8,128)(2,1)S(1)} %copy-done) | data formatting | bytes 786432
Async XLA Ops:
  34.3 1.8 %copy-start.2 = (bf16[512,384]{1,0:T(8,128)(2,1)S(1)}, bf16[512,384]{1,0:T(8,128)(2,1)}, u32[]{:S(2)}) copy-start(bf16[512,384]{1,0:T(8,128)(2,1)} %get-tuple-element.9) | copy-start | bytes 1179652
  36.1 1.1 %copy-start.1 = (bf16[512,384]{1,0:T(8,128)(2,1)S(1)}, bf16[512,384]{1,0:T(8,128)(2,1)}, u32[]{:S(2)}) copy-start(bf16[512,384]{1,0:T(8,128)(2,1)} %get-tuple-element.10) | copy-start | bytes 1179652
  37.3 1.1 %copy-start = (bf16[512,384]{1,0:T(8,128)(2,1)S(1)}, bf16[512,384]{1,0:T(8,128)(2,1)}, u32[]{:S(2)}) copy-start(bf16[512,384]{1,0:T(8,128)(2,1)} %get-tuple-element.11) | copy-start | bytes 1179652

commit v3 on v2

--- a/solution.py
+++ b/solution.py
@@ -237,6 +237,7 @@
     ]
     for load in loads:
         load.start()
+    lag = 3
     devices = 2 * inner
     zs = inner // 2
     groups = kv_far.shape[0]
@@ -490,21 +491,19 @@
         near_grads[head] = near_grads[head] + grad_kv[:near]
         part[head] = grad_kv[near:].reshape(2, inner, far, 2 * E).astype(jnp.bfloat16)
         core_copy(head).start()
-        if head >= 1:
-            reduce_core(head - 1)
-        if head >= 2:
-            reduce_x(head - 2)
-
-    reduce_core(heads - 1)
-    reduce_x(heads - 2)
+        if head >= lag:
+            reduce_core(head - lag)
+
+    for head in range(heads - lag, heads):
+        reduce_core(head)
     narrow(out_ref, vf)
-    reduce_x(heads - 1)
-    narrow(gq_ref, qf)
     for head in range(heads):
+        reduce_x(head)
         for index in range(1, stride // R1):
             piece = near_grads[head][index * far:(index + 1) * far]
             place(kf, head, index, piece, False)
             place(gf, head, index, piece, True)
+    narrow(gq_ref, qf)
     for head in range(heads):
         piece = near_grads[head][:far] + by_z[head, my_z].astype(jnp.float32)
         for step in range(1, zs):
@@ -523,6 +522,18 @@
             z_copy(head, step, my_z).wait_send()
 
 
+def store_kernel(*refs):
+    sources, targets, sems = refs[:4], refs[4:8], refs[8]
+    copies = [
+        pltpu.make_async_copy(source, target, sems.at[index])
+        for index, (source, target) in enumerate(zip(sources, targets))
+    ]
+    for copy in copies:
+        copy.start()
+    for copy in copies:
+        copy.wait()
+
+
 def slide_shards(queries, key_rows, value_rows, grad_out):
     rows, width = queries.shape
     heads = width // E
@@ -536,7 +547,7 @@
     bf16 = jnp.bfloat16
     whole = pl.BlockSpec(memory_space=pltpu.VMEM)
     dma = pltpu.SemaphoreType.DMA
-    return pl.pallas_call(
+    results = pl.pallas_call(
         functools.partial(slide_kernel, inner, heads, stride),
         out_shape=[jax.ShapeDtypeStruct((rows, width), bf16)] * 4,
         in_specs=[pl.BlockSpec(memory_space=pltpu.HBM)] * 4,
@@ -566,6 +577,13 @@
             collective_id=0, has_side_effects=True, vmem_limit_bytes=63 * 1024 * 1024
         ),
     )(queries, key_rows, value_rows, grad_out)
+    return pl.pallas_call(
+        store_kernel,
+        out_shape=[jax.ShapeDtypeStruct((rows, width), bf16)] * 4,
+        in_specs=[whole] * 4,
+        out_specs=[pl.BlockSpec(memory_space=pltpu.HBM)] * 4,
+        scratch_shapes=[dma((4,))],
+    )(*results)
 
 
 def shards(queries, key_rows, value_rows, grad_out):

time: 39.4 us -> 33.6 us (0.85)
  local copies, waits for them, and re-layouts: 4.85 us -> 0 us
  Pallas kernels: 33.6 us -> 32.8 us
    unnamed x10 -> x0, local copies, waits for them, and re-layouts: 4.85 us -> none
    pallas_call x1, Pallas kernels: 33.6 us -> 30.3 us  [slide_shards(): pl.pallas_call(functools.partial(slide_kernel, inner, heads, stride), out...]
    pallas_call x0 -> x1, Pallas kernels: none -> 2.52 us  [slide_shards(): pl.pallas_call(store_kernel, out_shape=[jax.ShapeDtypeStruct((rows, width...]
where the time goes in v3:
time: 33.6 us; the launch traced here: 33.4 us
  Pallas kernels  32.8 us (98%)
  between operations  0.64 us (2%)
    pallas_call x1, Pallas kernels, slide_shards(): pl.pallas_call(functools.partial(slide_kernel, inner, heads, stride), out...  30.3 us
    pallas_call x1, Pallas kernels, slide_shards(): pl.pallas_call(store_kernel, out_shape=[jax.ShapeDtypeStruct((rows, width...  2.52 us

profile of v3, /device:TPU:0, one launch (start us, length us, event | category | flops | bytes accessed | tf_op | source)
XLA Modules:
  0.0 33.4 jit_solution(17527645624272957102)
XLA Ops:
  0.6 30.3 %shard_map.75 = (bf16[512,384]{1,0:T(8,128)(2,1)}, bf16[512,384]{1,0:T(8,128)(2,1)}, bf16[512,384]{1,0:T(8,128)(2,1)}, bf16[512,384]{1,0:T(8,128)(2,1)}) custom-call(bf16[512,384]{1,0:T(8,128)(2,1)} %q_hbm.1, bf16[512,384]{1,0:T(8,128)(2,1)} %k_hbm.1, bf16[512,384]{1,0:T(8,128)(2,1)} %v_hbm.1, bf16[512,384]{1,0:T(8,128)(2,1)} %g_hbm.1), custom_call_target="tpu_custom_call" | custom-call | tf_op jit(solution)/shard_map/pallas_call | solution.py:550
  30.9 2.5 %shard_map.76 = (bf16[512,384]{1,0:T(8,128)(2,1)}, bf16[512,384]{1,0:T(8,128)(2,1)}, bf16[512,384]{1,0:T(8,128)(2,1)}, bf16[512,384]{1,0:T(8,128)(2,1)}) custom-call(bf16[512,384]{1,0:T(8,128)(2,1)} %get-tuple-element.8.refs_0_, bf16[512,384]{1,0:T(8,128)(2,1)} %get-tuple-element.9.refs_1_, bf16[512,384]{1,0:T(8,128)(2,1)} %get-tuple-element.10.refs_2_, ...), custom_call_target="tpu_custom_call" | custom-call | tf_op jit(solution)/shard_map/pallas_call | solution.py:580

commit v4 on v3

--- a/solution.py
+++ b/solution.py
@@ -237,7 +237,9 @@
     ]
     for load in loads:
         load.start()
-    lag = 3
+    lag = 1
+    early = 0
+    bundles, batch = part.shape[0], part.shape[2]
     devices = 2 * inner
     zs = inner // 2
     groups = kv_far.shape[0]
@@ -297,8 +299,6 @@
         kv_near[head, pl.ds(0, far), :] = block
         kv_far[head // group_heads, me, head % group_heads] = block
 
-    pl.semaphore_wait(barrier, len(neighbours))
-
     def block_id(core, z, x):
         return core * inner + 2 * z + x
 
@@ -349,9 +349,6 @@
         for step in range(zs):
             for x in (my_x, 1 - my_x):
                 await_block(group, block_id(1 - outer_id, peer_z(step), x))
-
-    for group in range(groups):
-        send_own(group)
 
     loads[2].wait()
     widen(qf, q_ref)
@@ -413,11 +410,8 @@
         ref[head // 2, pl.ds(offset, far, stride=stride), :] = kept
 
     near_grads = []
-    handing = [(pass_z, group) for group in range(groups)] + [(pass_x, group) for group in range(groups)]
-    for head in range(heads):
-        while len(handing) * heads > 2 * groups * (heads - 1 - head):
-            step, group = handing.pop(0)
-            step(group)
+
+    def near_head(head):
         keys = kv_near[head]
         q_only, g_only = split(qg_near[head, pl.ds(far, near - far), :])
         result, grad_q, grad_kv = attend(q_only, g_only, [keys], None)
@@ -427,6 +421,21 @@
             place(qf, head, index, grad_q[rows_in], False)
         near_grads.append(grad_kv)
 
+    for head in range(early):
+        near_head(head)
+    pl.semaphore_wait(barrier, len(neighbours))
+    for group in range(groups):
+        send_own(group)
+    handing = [(pass_z, group) for group in range(groups)] + [(pass_x, group) for group in range(groups)]
+    late = heads - early
+    for head in range(late):
+        near_head(early + head)
+        while len(handing) * late > 2 * groups * (late - 1 - head):
+            step, group = handing.pop(0)
+            step(group)
+    for step, group in handing:
+        step(group)
+
     total = devices * far
     row_id = lax.broadcasted_iota(jnp.int32, (far, near + total), 0)
     col_id = lax.broadcasted_iota(jnp.int32, (far, near + total), 1)
@@ -434,50 +443,52 @@
     twice = (col_id >= near) & (row_id % ratio == 0) & ((col_id - near) % ratio == 0)
     counts = jnp.where(twice, 2.0, 1.0)
 
-    def core_copy(head):
+    def core_copy(bundle):
         return pltpu.make_async_remote_copy(
-            src_ref=part.at[head, 1 - outer_id],
-            dst_ref=from_core.at[head],
-            send_sem=send_core.at[head],
-            recv_sem=recv_core.at[head],
+            src_ref=part.at[bundle, 1 - outer_id],
+            dst_ref=from_core.at[bundle],
+            send_sem=send_core.at[bundle],
+            recv_sem=recv_core.at[bundle],
             device_id=to_core,
             device_id_type=MESH,
         )
 
-    def x_copy(head):
+    def x_copy(bundle):
         return pltpu.make_async_remote_copy(
-            src_ref=by_x.at[head, 1 - my_x],
-            dst_ref=from_x.at[head],
-            send_sem=send_x.at[head],
-            recv_sem=recv_x.at[head],
+            src_ref=by_x.at[bundle, 1 - my_x],
+            dst_ref=from_x.at[bundle],
+            send_sem=send_x.at[bundle],
+            recv_sem=recv_x.at[bundle],
             device_id=to_x,
             device_id_type=MESH,
         )
 
-    def z_copy(head, step, slot):
+    def z_copy(bundle, step, slot):
         return pltpu.make_async_remote_copy(
-            src_ref=by_z.at[head, peer_z(step)],
-            dst_ref=from_z.at[head, slot],
-            send_sem=send_z.at[head, step],
-            recv_sem=recv_z.at[head, slot],
+            src_ref=by_z.at[bundle, peer_z(step)],
+            dst_ref=from_z.at[bundle, slot],
+            send_sem=send_z.at[bundle, step],
+            recv_sem=recv_z.at[bundle, slot],
             device_id=to_z(step),
             device_id_type=MESH,
         )
 
-    def reduce_core(head):
-        core_copy(head).wait_recv()
-        both = part[head, outer_id].astype(jnp.float32) + from_core[head].astype(jnp.float32)
-        both = both.astype(jnp.bfloat16).reshape(zs, 2, far, 2 * E)
+    def reduce_core(bundle):
+        core_copy(bundle).wait_recv()
+        both = part[bundle, outer_id].astype(jnp.float32) + from_core[bundle].astype(jnp.float32)
+        both = both.astype(jnp.bfloat16).reshape(batch, zs, 2, far, 2 * E)
         for x in range(2):
-            by_x[head, x] = both[:, x]
-        x_copy(head).start()
-
-    def reduce_x(head):
-        x_copy(head).wait_recv()
-        both = by_x[head, my_x].astype(jnp.float32) + from_x[head].astype(jnp.float32)
-        by_z[head] = both.astype(jnp.bfloat16)
+            by_x[bundle, x] = both[:, :, x]
+        x_copy(bundle).start()
+
+    def reduce_x(bundle):
+        x_copy(bundle).wait_recv()
+        both = by_x[bundle, my_x].astype(jnp.float32) + from_x[bundle].astype(jnp.float32)
+        both = both.astype(jnp.bfloat16)
+        for inside in range(batch):
+            by_z[bundle, :, inside] = both[inside]
         for step in range(1, zs):
-            z_copy(head, step, my_z).start()
+            z_copy(bundle, step, my_z).start()
 
     for head in range(heads):
         if head % group_heads == 0:
@@ -489,37 +500,43 @@
         place(vf, head, 0, result, True)
         place(qf, head, 0, grad_q, False)
         near_grads[head] = near_grads[head] + grad_kv[:near]
-        part[head] = grad_kv[near:].reshape(2, inner, far, 2 * E).astype(jnp.bfloat16)
-        core_copy(head).start()
-        if head >= lag:
-            reduce_core(head - lag)
-
-    for head in range(heads - lag, heads):
-        reduce_core(head)
+        part[head // batch, :, head % batch] = (
+            grad_kv[near:].reshape(2, inner, far, 2 * E).astype(jnp.bfloat16)
+        )
+        if head % batch == batch - 1:
+            core_copy(head // batch).start()
+            if head // batch >= lag:
+                reduce_core(head // batch - lag)
+
+    for bundle in range(max(0, bundles - lag), bundles):
+        reduce_core(bundle)
     narrow(out_ref, vf)
     for head in range(heads):
-        reduce_x(head)
+        if head % batch == 0:
+            reduce_x(head // batch)
         for index in range(1, stride // R1):
             piece = near_grads[head][index * far:(index + 1) * far]
             place(kf, head, index, piece, False)
             place(gf, head, index, piece, True)
     narrow(gq_ref, qf)
     for head in range(heads):
-        piece = near_grads[head][:far] + by_z[head, my_z].astype(jnp.float32)
+        bundle, inside = head // batch, head % batch
+        piece = near_grads[head][:far] + by_z[bundle, my_z, inside].astype(jnp.float32)
         for step in range(1, zs):
-            z_copy(head, step, peer_z(step)).wait_recv()
-            piece = piece + from_z[head, peer_z(step)].astype(jnp.float32)
+            if inside == 0:
+                z_copy(bundle, step, peer_z(step)).wait_recv()
+            piece = piece + from_z[bundle, peer_z(step), inside].astype(jnp.float32)
         place(kf, head, 0, piece, False)
         place(gf, head, 0, piece, True)
     narrow(gk_ref, kf)
     narrow(gv_ref, gf)
     for copy in pending:
         copy.wait_send()
-    for head in range(heads):
-        core_copy(head).wait_send()
-        x_copy(head).wait_send()
+    for bundle in range(bundles):
+        core_copy(bundle).wait_send()
+        x_copy(bundle).wait_send()
         for step in range(1, zs):
-            z_copy(head, step, my_z).wait_send()
+            z_copy(bundle, step, my_z).wait_send()
 
 
 def store_kernel(*refs):
@@ -543,7 +560,9 @@
     stride = rows * devices // KEYS
     far = rows // stride
     near = rows // R1
-    groups = 2
+    groups = 3
+    batch = 2
+    bundles = heads // batch
     bf16 = jnp.bfloat16
     whole = pl.BlockSpec(memory_space=pltpu.VMEM)
     dma = pltpu.SemaphoreType.DMA
@@ -558,20 +577,20 @@
         + [pltpu.VMEM((heads, near, 2 * E), bf16)] * 2
         + [
             pltpu.VMEM((groups, devices, heads // groups, far, 2 * E), bf16),
-            pltpu.VMEM((heads, 2, inner, far, 2 * E), bf16),
-            pltpu.VMEM((heads, inner, far, 2 * E), bf16),
-            pltpu.VMEM((heads, 2, zs, far, 2 * E), bf16),
-            pltpu.VMEM((heads, zs, far, 2 * E), bf16),
-            pltpu.VMEM((heads, zs, far, 2 * E), bf16),
-            pltpu.VMEM((heads, zs, far, 2 * E), bf16),
+            pltpu.VMEM((bundles, 2, batch, inner, far, 2 * E), bf16),
+            pltpu.VMEM((bundles, batch, inner, far, 2 * E), bf16),
+            pltpu.VMEM((bundles, 2, batch, zs, far, 2 * E), bf16),
+            pltpu.VMEM((bundles, batch, zs, far, 2 * E), bf16),
+            pltpu.VMEM((bundles, zs, batch, far, 2 * E), bf16),
+            pltpu.VMEM((bundles, zs, batch, far, 2 * E), bf16),
             dma((groups, 4 * zs)),
             dma((groups, devices)),
-            dma((heads,)),
-            dma((heads,)),
-            dma((heads,)),
-            dma((heads,)),
-            dma((heads, zs)),
-            dma((heads, zs)),
+            dma((bundles,)),
+            dma((bundles,)),
+            dma((bundles,)),
+            dma((bundles,)),
+            dma((bundles, zs)),
+            dma((bundles, zs)),
         ],
         compiler_params=pltpu.CompilerParams(
             collective_id=0, has_side_effects=True, vmem_limit_bytes=63 * 1024 * 1024

time: 33.6 us -> 32.4 us (0.964)
  Pallas kernels: 32.8 us -> 31.6 us
    pallas_call x1, Pallas kernels: 30.3 us -> 29.1 us  [slide_shards(): pl.pallas_call(functools.partial(slide_kernel, inner, heads, stride), out...]
where the time goes in v4:
time: 32.4 us; the launch traced here: 32.2 us
  Pallas kernels  31.6 us (98%)
  between operations  0.64 us (2%)
    pallas_call x1, Pallas kernels, slide_shards(): pl.pallas_call(functools.partial(slide_kernel, inner, heads, stride), out...  29.1 us
    pallas_call x1, Pallas kernels, slide_shards(): pl.pallas_call(store_kernel, out_shape=[jax.ShapeDtypeStruct((rows, width...  2.52 us

profile of v4, /device:TPU:0, one launch (start us, length us, event | category | flops | bytes accessed | tf_op | source)
XLA Modules:
  0.0 32.2 jit_solution(628351631954828107)
XLA Ops:
  0.6 29.1 %shard_map.75 = (bf16[512,384]{1,0:T(8,128)(2,1)}, bf16[512,384]{1,0:T(8,128)(2,1)}, bf16[512,384]{1,0:T(8,128)(2,1)}, bf16[512,384]{1,0:T(8,128)(2,1)}) custom-call(bf16[512,384]{1,0:T(8,128)(2,1)} %q_hbm.1, bf16[512,384]{1,0:T(8,128)(2,1)} %k_hbm.1, bf16[512,384]{1,0:T(8,128)(2,1)} %v_hbm.1, bf16[512,384]{1,0:T(8,128)(2,1)} %g_hbm.1), custom_call_target="tpu_custom_call" | custom-call | tf_op jit(solution)/shard_map/pallas_call | solution.py:569
  29.7 2.5 %shard_map.76 = (bf16[512,384]{1,0:T(8,128)(2,1)}, bf16[512,384]{1,0:T(8,128)(2,1)}, bf16[512,384]{1,0:T(8,128)(2,1)}, bf16[512,384]{1,0:T(8,128)(2,1)}) custom-call(bf16[512,384]{1,0:T(8,128)(2,1)} %get-tuple-element.8.refs_0_, bf16[512,384]{1,0:T(8,128)(2,1)} %get-tuple-element.9.refs_1_, bf16[512,384]{1,0:T(8,128)(2,1)} %get-tuple-element.10.refs_2_, ...), custom_call_target="tpu_custom_call" | custom-call | tf_op jit(solution)/shard_map/pallas_call | solution.py:599

commit v5 on v4

--- a/solution.py
+++ b/solution.py
@@ -286,9 +286,12 @@
         for pair in range(pairs):
             wide[pair] = ref[:, pl.ds(pair * 2 * E, 2 * E)].astype(jnp.float32)
 
+    def narrow_pair(ref, wide, pair):
+        ref[:, pl.ds(pair * 2 * E, 2 * E)] = wide[pair].astype(jnp.bfloat16)
+
     def narrow(ref, wide):
         for pair in range(pairs):
-            ref[:, pl.ds(pair * 2 * E, 2 * E)] = wide[pair].astype(jnp.bfloat16)
+            narrow_pair(ref, wide, pair)
 
     loads[0].wait()
     widen(kf, k_ref)
@@ -528,8 +531,9 @@
             piece = piece + from_z[bundle, peer_z(step), inside].astype(jnp.float32)
         place(kf, head, 0, piece, False)
         place(gf, head, 0, piece, True)
-    narrow(gk_ref, kf)
-    narrow(gv_ref, gf)
+        if head % 2 == 1:
+            narrow_pair(gk_ref, kf, head // 2)
+            narrow_pair(gv_ref, gf, head // 2)
     for copy in pending:
         copy.wait_send()
     for bundle in range(bundles):

time: 32.4 us -> 32.4 us (level)
  no operation moved by 1% of the time
where the time goes in v5:
time: 32.4 us; the launch traced here: 32.2 us
  Pallas kernels  31.6 us (98%)
  between operations  0.64 us (2%)
    pallas_call x1, Pallas kernels, slide_shards(): pl.pallas_call(functools.partial(slide_kernel, inner, heads, stride), out...  29.1 us
    pallas_call x1, Pallas kernels, slide_shards(): pl.pallas_call(store_kernel, out_shape=[jax.ShapeDtypeStruct((rows, width...  2.52 us

profile of v5, /device:TPU:0, one launch (start us, length us, event | category | flops | bytes accessed | tf_op | source)
XLA Modules:
  0.0 32.2 jit_solution(17487323480536861179)
XLA Ops:
  0.6 29.1 %shard_map.75 = (bf16[512,384]{1,0:T(8,128)(2,1)}, bf16[512,384]{1,0:T(8,128)(2,1)}, bf16[512,384]{1,0:T(8,128)(2,1)}, bf16[512,384]{1,0:T(8,128)(2,1)}) custom-call(bf16[512,384]{1,0:T(8,128)(2,1)} %q_hbm.1, bf16[512,384]{1,0:T(8,128)(2,1)} %k_hbm.1, bf16[512,384]{1,0:T(8,128)(2,1)} %v_hbm.1, bf16[512,384]{1,0:T(8,128)(2,1)} %g_hbm.1), custom_call_target="tpu_custom_call" | custom-call | tf_op jit(solution)/shard_map/pallas_call | solution.py:573
  29.7 2.5 %shard_map.76 = (bf16[512,384]{1,0:T(8,128)(2,1)}, bf16[512,384]{1,0:T(8,128)(2,1)}, bf16[512,384]{1,0:T(8,128)(2,1)}, bf16[512,384]{1,0:T(8,128)(2,1)}) custom-call(bf16[512,384]{1,0:T(8,128)(2,1)} %get-tuple-element.8.refs_0_, bf16[512,384]{1,0:T(8,128)(2,1)} %get-tuple-element.9.refs_1_, bf16[512,384]{1,0:T(8,128)(2,1)} %get-tuple-element.10.refs_2_, ...), custom_call_target="tpu_custom_call" | custom-call | tf_op jit(solution)/shard_map/pallas_call | solution.py:603
